TPU v7x, 32 devices: a whole 2x2x4 slice. The times are simulated.
32 devices in a mesh: grp: 2 (over y), freq: 4 (over z), shot: 2 (over x), rcv: 2 (over core).
Axes of the slice: x: 2, y: 2, z: 4, core: 2. Of those that a mesh axis runs over, the one named last changes fastest.
Arguments:
- data: bfloat16 [2, 256, 32, 4096], P(None, 'freq', ('grp', 'shot'), 'rcv'), parts along dimension 2, may hold values from -6 to 6
- estimate: bfloat16 [2, 256, 32, 4096], P(None, 'freq', ('grp', 'shot'), 'rcv'), parts along dimension 2, may hold values from -0.09375 to 0.09375
- window_data: bfloat16 [2, 256, 32, 16], P(None, 'freq', ('grp', 'shot')), parts along dimension 2, may hold values from -6 to 6
- wavelet: float32 [2, 512], P(None, ('grp', 'freq')), parts along dimension 1, may hold values from -24 to 24
- positions: int32 [32], P(('grp', 'shot')), parts along dimension 0, may hold values from 0 to 4095
- bins: int32 [512], P('grp'), parts along dimension 0, may hold values from 0 to 399
- threshold: int32 [2], P('grp'), parts along dimension 0, may hold values from 8 to 40
- step: float32 [2], P('grp'), parts along dimension 0, may hold values from 0.25 to 1
Outputs:
- primaries: bfloat16 [1024, 32, 4096], P('freq', ('grp', 'shot'), 'rcv'), parts along dimension 1
There are 2 independent parts, one for each index of `grp`. A program takes and returns all parts, laid end to end along the dimension named above; each array names one. Nothing has to cross between parts.
All inputs are finite; a program needn't handle non-finite values.
Results may differ from a plain program's by a relative error of at most 0.0059.
The roundings to bfloat16 on the way count: a program that leaves them out, or rounds other values in their place, can miss the bound.
Values may be sent and summed in bfloat16 or wider, within the bound.
A program may use at most 64 MiB of HBM per device.

v0:
```python
from functools import partial
import math
import jax
import jax.numpy as jnp
from jax import lax
from jax.sharding import PartitionSpec as P

NF = 256
RCV = 4096
NT = 1024


def make_down(lines, spots, wavelet, offset):
    width = lines.shape[3]
    columns = offset + lax.iota(jnp.int32, width)
    select = (columns[None, None, :] == spots[None, :, None]).astype(jnp.float32)
    down_re = (wavelet[0][:, None, None] * select - lines[0].astype(jnp.float32)).astype(
        jnp.bfloat16
    )
    down_im = (wavelet[1][:, None, None] * select - lines[1].astype(jnp.float32)).astype(
        jnp.bfloat16
    )
    return (down_re, down_im)


def body(data, estimate, window_data, wavelet, positions, bins, threshold, step):
    product = partial(jnp.einsum, preferred_element_type=jnp.float32)
    offset = lax.axis_index("rcv") * data.shape[3]
    shots_all = data.shape[2] * lax.axis_size("shot")
    norm = 1.0 / math.sqrt(shots_all * RCV)
    lines, spots = (
        lax.all_gather(data, "shot", axis=2, tiled=True),
        lax.all_gather(positions, "shot", axis=0, tiled=True),
    )
    down_re, down_im = make_down(lines, spots, wavelet, offset)
    rows_re = estimate[0]
    rows_im = estimate[1]
    model_re = product("frc,fsc->frs", rows_re, down_re) - product("frc,fsc->frs", rows_im, down_im)
    model_im = product("frc,fsc->frs", rows_re, down_im) + product("frc,fsc->frs", rows_im, down_re)
    model_re, model_im = lax.psum((model_re, model_im), "rcv")
    err_re = (window_data[0].astype(jnp.float32) - model_re).astype(jnp.bfloat16)
    err_im = (window_data[1].astype(jnp.float32) - model_im).astype(jnp.bfloat16)
    grad_re = product("frs,fsc->frc", err_re, down_re) + product("frs,fsc->frc", err_im, down_im)
    grad_im = product("frs,fsc->frc", err_im, down_re) - product("frs,fsc->frc", err_re, down_im)
    step_size = step[0]
    upd_re = (estimate[0].astype(jnp.float32) - step_size * (grad_re * norm)).astype(jnp.bfloat16)
    upd_im = (estimate[1].astype(jnp.float32) - step_size * (grad_im * norm)).astype(jnp.bfloat16)
    updated = jnp.stack([upd_re, upd_im], axis=0)
    n_freq = bins.shape[0]
    times = lax.iota(jnp.int32, NT)
    phase = bins[:, None] * times[None, :] % NT
    angle = 2.0 * math.pi / NT * phase.astype(jnp.float32)
    table = jnp.concatenate([jnp.cos(angle), -jnp.sin(angle)], axis=0).astype(jnp.bfloat16)
    level = threshold[0].astype(jnp.float32) / 64.0
    amplitude = math.sqrt(RCV / NF)
    piece = lax.all_to_all(updated, "freq", split_axis=3, concat_axis=1, tiled=True)
    row_count = piece.shape[2]
    col_count = piece.shape[3]
    stacked = piece.reshape(2 * n_freq, row_count * col_count)
    trace = (
        lax.dot_general(
            table, stacked, (((0,), (0,)), ((), ())), preferred_element_type=jnp.float32
        )
        * amplitude
    )
    sparse = (jnp.sign(trace) * jnp.maximum(jnp.abs(trace) - level, 0.0)).astype(jnp.bfloat16)
    sparse = sparse.reshape(NT, row_count, col_count)
    return lax.all_to_all(sparse, "freq", split_axis=0, concat_axis=2, tiled=True)


def solution(mesh):
    return jax.shard_map(
        body,
        mesh=mesh,
        in_specs=(
            P(None, "freq", ("grp", "shot"), "rcv"),
            P(None, "freq", ("grp", "shot"), "rcv"),
            P(None, "freq", ("grp", "shot"), None),
            P(None, ("grp", "freq")),
            P(("grp", "shot")),
            P("grp"),
            P("grp"),
            P("grp"),
        ),
        out_specs=P("freq", ("grp", "shot"), "rcv"),
        check_vma=False,
    )
```

profile of v0, /device:TPU:0, one launch (start us, length us, event | category | flops | bytes accessed | tf_op | source)
XLA Modules:
  0.0 535.6 jit_solution(10995999869594317697)
XLA Ops:
  6.5 0.0 all-gather.2.cloned.1.call-start
  6.5 0.7 all-gather.2.cloned.1.call-update
  7.3 0.0 all-reduce.4.cloned.1.call-start
  7.3 0.0 copy-done.12
  7.3 0.6 dynamic-slice
  8.6 0.0 copy-done.11
  8.6 0.2 dynamic-update-slice
  8.8 5.2 all-reduce
  14.0 0.0 copy-done.10
  14.0 0.1 compare_convert_fusion
  14.1 101.5 %all-gather.2.cloned.1.call-done = bf16[2,64,16,2048]{3,2,1,0:T(8,128)(2,1)} async-done(((bf16[2,64,8,2048]{3,2,1,0:T(8,128)(2,1)}), bf16[2,64,16,2048]{3,2,1,0:T(8,128)(2,1)}) %all-gather.2.cloned.1.call-update) | async-done | bytes 8388624 | tf_op jit(solution)/shard_map/all_gather | solution.py:32
  115.6 5.3 fusion
  121.0 0.0 copy-start.2
  121.0 0.0 copy-start
  121.0 0.0 copy-done.4
  121.0 1.6 fusion.6
  122.6 1.6 fusion.4
  124.1 0.0 copy-done.2
  124.1 2.3 fusion.19
  126.4 0.0 copy-done
  126.4 1.9 fusion.25
  128.3 0.0 all-reduce.4.cloned.1.call-update
  128.4 0.0 copy-done.8
  128.4 0.1 copy.26
  128.5 0.1 copy.27
  129.3 18.0 %all-reduce.4.cloned.1.call-done = (f32[64,8,16]{2,1,0:T(8,128)}, f32[64,8,16]{2,1,0:T(8,128)}) async-done(((f32[64,8,16]{2,1,0:T(8,128)}, f32[64,8,16]{2,1,0:T(8,128)}), (f32[64,8,16]{2,1,0:T(8,128)}, f32[64,8,16]{2,1,0:T(8,128)})) %all-reduce.4.cloned.1.call-update) | async-done | bytes 65552 | tf_op jit(solution)/shard_map/psum | solution.py:40
  147.3 3.1 fusion.41
  150.4 0.4 copy-done.3
  150.8 0.0 copy-done.7
  150.9 0.7 fusion.43
  151.6 1.5 copy-done.1
  153.1 1.3 copy-done.5
  154.3 1.0 fusion.2
  155.3 0.0 copy-done.6
  155.3 1.0 fusion.3
  156.3 2.3 pad_maximum_fusion
  158.6 13.2 %copy.23 = bf16[2,64,8,2048]{1,2,0,3:T(8,128)(2,1)} copy(bf16[2,64,8,2048]{3,2,1,0:T(8,128)(2,1)} %pad_maximum_fusion) | data formatting | bytes 8388608 | tf_op jit(solution)/shard_map/stack | solution.py:48
  171.8 9.6 %reshape.71 = bf16[4,2,262144]{2,1,0:T(2,128)(2,1)} reshape(bf16[2048,2,8,64]{3,2,1,0:T(8,128)(2,1)} %bitcast.77) | data formatting | bytes 8388608
  181.4 5.0 all-to-all-start
  187.1 4.9 cosine_convert_fusion
  191.9 88.4 %all-to-all-done = bf16[4,2,262144]{2,1,0:T(2,128)(2,1)} async-done(((bf16[4,2,262144]{2,1,0:T(2,128)(2,1)}), bf16[4,2,262144]{2,1,0:T(2,128)(2,1)}, u32[]{:S(2)}, u32[]{:S(2)}) %all-to-all-start) | async-done | bytes 4194336 | tf_op jit(solution)/shard_map/all_to_all | solution.py:56
  280.3 9.3 %reshape.72 = bf16[2048,2,8,64]{3,2,1,0:T(8,128)(2,1)} reshape(bf16[4,2,262144]{2,1,0:T(2,128)(2,1)} %all-to-all-done) | data formatting | bytes 8388608
  289.6 12.0 %copy.24 = bf16[2,64,8,4,512]{4,2,1,3,0:T(8,128)(2,1)} copy(bf16[2,64,8,4,512]{1,2,0,4,3:T(8,128)(2,1)} %bitcast.78) | data formatting | bytes 8388608 | tf_op jit(solution)/shard_map/all_to_all | solution.py:56
  301.6 4.4 copy.28
  306.0 12.1 %multiply_convert_fusion = bf16[1024,4096]{1,0:T(8,128)(2,1)} fusion(bf16[512,4096]{1,0:T(8,128)(2,1)S(1)} %bitcast.83, f32[]{:T(128)} %bitcast.16, bf16[256,1024]{1,0:T(8,128)(2,1)S(1)} %get-tuple-element.12, bf16[256,1024]{1,0:T(8,128)(2,1)S(1)} %get-tuple-element.11), kind=kOutput, calls=%fused_computation | convolution fusion | flops 4326424576 | bytes 13631492 | tf_op jit(solution)/shard_map/dot_general | solution.py:61
  318.1 12.2 %copy.29 = bf16[128,8,8,512]{3,2,1,0:T(8,128)(2,1)} copy(bf16[128,8,8,512]{3,1,2,0:T(8,128)(2,1)} %bitcast.82) | data formatting | bytes 16777216
  330.3 190.4 %all_to_all.33 = bf16[1024,8,512]{2,1,0:T(8,128)(2,1)} all-to-all(bf16[1024,8,512]{2,1,0:T(8,128)(2,1)} %bitcast.79), channel_id=1, replica_groups=mesh['grp'=2,'freq'=4,'shot'=2,'rcv'=2] {'freq'}, dimensions={0} | all-to-all | bytes 16777216 | tf_op jit(solution)/shard_map/all_to_all | solution.py:68
  520.7 8.1 %copy.25 = bf16[4,256,8,512]{3,2,0,1:T(8,128)(2,1)} copy(bf16[4,256,8,512]{3,2,1,0:T(8,128)(2,1)} %bitcast.80) | data formatting | bytes 16777216 | tf_op jit(solution)/shard_map/all_to_all | solution.py:68
  (16 shorter events, 0.0 us)
Async XLA Ops:
  6.5 0.8 copy-start.12
  6.5 2.0 copy-start.11
  6.5 7.5 %copy-start.10 = (f32[2,64]{1,0:T(2,128)S(1)}, f32[2,64]{1,0:T(2,128)}, u32[]{:S(2)}) copy-start(f32[2,64]{1,0:T(2,128)} %param.11) | copy-start | bytes 1540
  6.5 109.1 %all-gather.2.cloned.1.call-start = ((), (), s32[]{:S(2)}) async-start(), calls=%async_computation.2 | async-start | bytes 12582912 | tf_op jit(solution)/shard_map/all_gather | solution.py:32
  7.3 140.1 %all-reduce.4.cloned.1.call-start = ((), (), s32[]{:S(2)}) async-start(), calls=%async_computation.3 | async-start | bytes 1048576 | tf_op jit(solution)/shard_map/psum | solution.py:40
  115.6 5.3 copy-start.4
  121.0 3.2 copy-start.2
  121.0 5.5 %copy-start = (bf16[64,16,2048]{2,1,0:T(8,128)(2,1)}, bf16[64,16,2048]{2,1,0:T(8,128)(2,1)S(1)}, u32[]{:S(2)}) copy-start(bf16[64,16,2048]{2,1,0:T(8,128)(2,1)S(1)} %get-tuple-element.7) | copy-start | bytes 12582916
  126.4 1.9 copy-start.8
  147.3 3.5 copy-start.3
  147.3 3.5 copy-start.7
  150.9 2.2 copy-start.1
  150.9 3.5 copy-start.5
  154.3 1.0 copy-start.6
  181.4 5.7 %copy-start.9 = (s32[256]{0:T(256)S(1)}, s32[256]{0:T(256)}, u32[]{:S(2)}) copy-start(s32[256]{0:T(256)} %param.13) | copy-start | bytes 3076
  181.4 99.0 %all-to-all-start = ((bf16[4,2,262144]{2,1,0:T(2,128)(2,1)}), bf16[4,2,262144]{2,1,0:T(2,128)(2,1)}, u32[]{:S(2)}, u32[]{:S(2)}) async-start(bf16[4,2,262144]{2,1,0:T(2,128)(2,1)} %reshape.71), calls=%async_computation | async-start | bytes 8388608 | tf_op jit(solution)/shard_map/all_to_all | solution.py:56
Sparse Core Ops, SparseCore 0:
  8.9 106.6 all-gather.1
  128.5 18.7 all-reduce.3
where the time goes:
time: 537 us; the launch traced here: 536 us
  waiting for transfers between devices  209 us (39%)
  blocking collectives  196 us (36%)
  local copies, waits for them, and re-layouts  73.1 us (14%)
  matrix products  25.2 us (5%)
  between operations  15.5 us (3%)
  other arithmetic  12.6 us (2%)
    all_to_all x1, blocking collectives, body(): lax.all_to_all(sparse, 'freq', split_axis=0, concat_axis=2, tiled=True)  190 us
    all_gather x1, waiting for transfers between devices, body(): lax.all_gather(data, 'shot', axis=2, tiled=True)  102 us
    all_to_all x1, waiting for transfers between devices, body(): lax.all_to_all(updated, 'freq', split_axis=3, concat_axis=1, tiled=True)  88.4 us
    unnamed x35, local copies, waits for them, and re-layouts  39.8 us
    psum x1, waiting for transfers between devices, body(): model_re, model_im = lax.psum((model_re, model_im), 'rcv')  18 us
    another operation x1, local copies, waits for them, and re-layouts, body(): updated = jnp.stack([upd_re, upd_im], axis=0)  13.2 us
    dot_general x1, matrix products, body(): lax.dot_general(table, stacked, (((0,), (0,)), ((), ())), preferred_eleme...  12.1 us
    all_to_all x1, local copies, waits for them, and re-layouts, body(): lax.all_to_all(updated, 'freq', split_axis=3, concat_axis=1, tiled=True)  12 us
  transfers between devices with their start and end apart: 3, of which 3 were waited for; matrix products, arithmetic and copies ran while one was open for 1% of the time, Pallas kernels for 0%

commit v1 on v0

--- a/solution.py
+++ b/solution.py
@@ -8,6 +8,18 @@
 NF = 256
 RCV = 4096
 NT = 1024
+
+
+def split_up(x, dim, peers):
+    shape = x.shape
+    pieces = x.reshape(*shape[:dim], peers, shape[dim] // peers, *shape[dim + 1 :])
+    return jnp.moveaxis(pieces, dim, 0)
+
+
+def joined_along(parts, dim):
+    parts = jnp.moveaxis(parts, 0, dim)
+    lengths = parts.shape
+    return parts.reshape(*lengths[:dim], lengths[dim] * lengths[dim + 1], *lengths[dim + 2 :])
 
 
 def make_down(lines, spots, wavelet, offset):
@@ -53,7 +65,14 @@
     table = jnp.concatenate([jnp.cos(angle), -jnp.sin(angle)], axis=0).astype(jnp.bfloat16)
     level = threshold[0].astype(jnp.float32) / 64.0
     amplitude = math.sqrt(RCV / NF)
-    piece = lax.all_to_all(updated, "freq", split_axis=3, concat_axis=1, tiled=True)
+    peers, here = (lax.axis_size("freq"), lax.axis_index("freq"))
+    blocks = split_up(updated, 3, peers)
+    gathered = [blocks[here]]
+    for lap in range(1, peers):
+        sent = blocks[here ^ lap]
+        gathered.append(lax.ppermute(sent, "freq", [(i, i ^ lap) for i in range(peers)]))
+    blocks = jnp.stack(gathered)[here ^ jnp.arange(peers)]
+    piece = joined_along(blocks, 1)
     row_count = piece.shape[2]
     col_count = piece.shape[3]
     stacked = piece.reshape(2 * n_freq, row_count * col_count)

time: 537 us -> 491 us (0.914)
  local copies, waits for them, and re-layouts: 73.1 us -> 34.5 us
  waiting for transfers between devices: 209 us -> 184 us
  blocking collectives: 196 us -> 214 us
    all_to_all x1 -> x0, waiting for transfers between devices: 88.4 us -> none  [body(): lax.all_to_all(updated, 'freq', split_axis=3, concat_axis=1, tiled=True)]
    ppermute x0 -> x3, waiting for transfers between devices: none -> 63.7 us  [body(): lax.ppermute(sent, 'freq', [(i, i ^ lap) for i in range(peers)])]
    unnamed x35 -> x33, local copies, waits for them, and re-layouts: 39.8 us -> 18.8 us
    all_to_all x1, blocking collectives: 190 us -> 209 us  [body(): lax.all_to_all(sparse, 'freq', split_axis=0, concat_axis=2, tiled=True)]
    another operation x1 -> x0, local copies, waits for them, and re-layouts: 13.2 us -> none  [body(): updated = jnp.stack([upd_re, upd_im], axis=0)]
    all_to_all x1 -> x0, local copies, waits for them, and re-layouts: 12 us -> none  [body(): lax.all_to_all(updated, 'freq', split_axis=3, concat_axis=1, tiled=True)]
  transfers between devices with their start and end apart: 3 -> 5, of which waited for: 3 -> 4; matrix products, arithmetic and copies ran while one was open for 1% -> 1% of each run, Pallas kernels for 0% -> 0%
where the time goes in v1:
time: 491 us
  blocking collectives  214 us (44%)
  waiting for transfers between devices  184 us (37%)
  local copies, waits for them, and re-layouts  34.5 us (7%)
  matrix products  25.2 us (5%)
  between operations  15.6 us (3%)
  other arithmetic  12.9 us (3%)
    all_to_all x1, blocking collectives, body(): lax.all_to_all(sparse, 'freq', split_axis=0, concat_axis=2, tiled=True)  209 us
    all_gather x1, waiting for transfers between devices, body(): lax.all_gather(data, 'shot', axis=2, tiled=True)  102 us
    ppermute x3, waiting for transfers between devices, body(): lax.ppermute(sent, 'freq', [(i, i ^ lap) for i in range(peers)])  63.7 us
    unnamed x33, local copies, waits for them, and re-layouts  18.8 us
    psum x1, waiting for transfers between devices, body(): model_re, model_im = lax.psum((model_re, model_im), 'rcv')  18 us
    dot_general x1, matrix products, body(): lax.dot_general(table, stacked, (((0,), (0,)), ((), ())), preferred_eleme...  12.1 us
  transfers between devices with their start and end apart: 5, of which 4 were waited for; matrix products, arithmetic and copies ran while one was open for 1% of the time, Pallas kernels for 0%

profile of v1, /device:TPU:0, one launch (start us, length us, event | category | flops | bytes accessed | tf_op | source)
XLA Modules:
  0.0 490.5 jit_solution(17897116190748681745)
XLA Ops:
  6.5 0.0 all-gather.2.cloned.1.call-start
  6.5 0.7 all-gather.2.cloned.1.call-update
  7.3 0.0 all-reduce.4.cloned.1.call-start
  7.3 0.0 copy-done.12
  7.3 0.6 dynamic-slice.16
  8.6 0.0 copy-done.11
  8.6 0.2 dynamic-update-slice
  8.8 5.2 %all-reduce = s32[16]{0:T(128)S(1)} all-reduce(s32[16]{0:T(128)S(1)} %dynamic-update-slice), channel_id=1, replica_groups=mesh['grp'=2,'freq'=4,'shot'=2,'rcv'=2] {'shot'}, use_global_device_ids=true, to_apply=%add | all-reduce | flops 16 | bytes 128
  14.0 0.0 copy-done.10
  14.0 0.1 compare_convert_fusion
  14.1 101.5 %all-gather.2.cloned.1.call-done = bf16[2,64,16,2048]{3,2,1,0:T(8,128)(2,1)} async-done(((bf16[2,64,8,2048]{3,2,1,0:T(8,128)(2,1)}), bf16[2,64,16,2048]{3,2,1,0:T(8,128)(2,1)}) %all-gather.2.cloned.1.call-update) | async-done | bytes 8388624 | tf_op jit(solution)/shard_map/all_gather | solution.py:44
  115.6 5.3 %fusion = (bf16[64,16,2048]{2,1,0:T(8,128)(2,1)S(1)}, bf16[64,16,2048]{2,1,0:T(8,128)(2,1)S(1)}) fusion(bf16[2,64,16,2048]{3,2,1,0:T(8,128)(2,1)} %all-gather.2.cloned.1.call-done, f32[64]{0:T(128)S(1)} %get-tuple-element.17, f32[16,2048]{1,0:T(8,128)S(1)} %compare_convert_fusion, f32[64]{0:T(128)S(1)} %get-tuple-element.18), kind=kLoop, calls=%fused_computation.3 | loop fusion | flops 16777216 | bytes 16908800 | tf_op jit(solution)/shard_map/convert_element_type | solution.py:32
  121.0 0.0 copy-start.2
  121.0 0.0 copy-done.4
  121.0 1.6 fusion.2
  122.6 1.6 fusion.4
  124.1 1.9 fusion.23
  126.1 0.0 copy-done.2
  126.1 2.3 fusion.17
  128.3 0.0 all-reduce.4.cloned.1.call-update
  128.4 0.1 copy.20
  128.6 0.1 copy.19
  129.4 18.0 %all-reduce.4.cloned.1.call-done = (f32[64,8,16]{2,1,0:T(8,128)}, f32[64,8,16]{2,1,0:T(8,128)}) async-done(((f32[64,8,16]{2,1,0:T(8,128)}, f32[64,8,16]{2,1,0:T(8,128)}), (f32[64,8,16]{2,1,0:T(8,128)}, f32[64,8,16]{2,1,0:T(8,128)})) %all-reduce.4.cloned.1.call-update) | async-done | bytes 65552 | tf_op jit(solution)/shard_map/psum | solution.py:52
  147.3 3.1 fusion.50
  150.4 0.4 copy-done.3
  150.8 0.0 copy-done.7
  150.9 0.7 fusion.48
  151.6 1.5 copy-done.1
  153.1 1.3 copy-done.5
  154.3 1.0 subtract_convert_fusion
  155.3 1.0 subtract_convert_fusion.1
  156.3 0.0 copy-start.9
  156.3 0.4 fusion.32
  156.7 1.8 collective-permute-start
  158.5 2.4 collective-permute-start.1
  160.9 0.2 collective-permute-start.2
  161.8 4.9 cosine_convert_fusion
  166.7 37.3 %collective-permute-done = bf16[2,64,8,512]{3,2,1,0:T(8,128)(2,1)S(1)} collective-permute-done((bf16[2,64,8,512]{3,2,1,0:T(8,128)(2,1)S(1)}, bf16[2,64,8,512]{3,2,1,0:T(8,128)(2,1)S(1)}, u32[]{:S(2)}, u32[]{:S(2)}) %collective-permute-start) | collective-permute-done | bytes 1048608 | tf_op jit(solution)/shard_map/ppermute | solution.py:73
  204.0 26.4 %collective-permute-done.1 = bf16[2,64,8,512]{3,2,1,0:T(8,128)(2,1)S(1)} collective-permute-done((bf16[2,64,8,512]{3,2,1,0:T(8,128)(2,1)S(1)}, bf16[2,64,8,512]{3,2,1,0:T(8,128)(2,1)S(1)}, u32[]{:S(2)}, u32[]{:S(2)}) %collective-permute-start.1) | collective-permute-done | bytes 1048608 | tf_op jit(solution)/shard_map/ppermute | solution.py:73
  230.4 0.0 collective-permute-done.2
  230.4 2.3 pad_maximum_fusion
  232.7 4.9 %gather_fusion = bf16[4,2,64,8,512]{4,3,2,1,0:T(8,128)(2,1)} fusion(bf16[4,2,64,8,512]{4,3,2,1,0:T(8,128)(2,1)} %pad_maximum_fusion, s32[1024]{0:T(1024)S(1)} %pad_clamp_fusion), kind=kCustom, calls=%fused_computation | custom fusion | bytes 8388624 | tf_op jit(solution)/shard_map/gather | solution.py:74
  237.6 2.6 copy.17
  240.3 2.2 copy.21
  242.5 12.1 %multiply_convert_fusion = bf16[1024,4096]{1,0:T(8,128)(2,1)} fusion(bf16[512,4096]{1,0:T(8,128)(2,1)S(1)} %bitcast.92, f32[]{:T(128)} %bitcast.23, bf16[256,1024]{1,0:T(8,128)(2,1)S(1)} %get-tuple-element.16, bf16[256,1024]{1,0:T(8,128)(2,1)S(1)} %get-tuple-element.15), kind=kOutput, calls=%fused_computation.1 | convolution fusion | flops 4326424576 | bytes 13631492 | tf_op jit(solution)/shard_map/dot_general | solution.py:80
  254.6 12.2 %copy.22 = bf16[128,8,8,512]{3,2,1,0:T(8,128)(2,1)} copy(bf16[128,8,8,512]{3,1,2,0:T(8,128)(2,1)} %bitcast.91) | data formatting | bytes 16777216
  266.8 208.8 %all_to_all.18 = bf16[1024,8,512]{2,1,0:T(8,128)(2,1)} all-to-all(bf16[1024,8,512]{2,1,0:T(8,128)(2,1)} %bitcast.85), channel_id=1, replica_groups=mesh['grp'=2,'freq'=4,'shot'=2,'rcv'=2] {'freq'}, dimensions={0} | all-to-all | bytes 16777216 | tf_op jit(solution)/shard_map/all_to_all | solution.py:87
  475.6 8.1 %copy.18 = bf16[4,256,8,512]{3,2,0,1:T(8,128)(2,1)} copy(bf16[4,256,8,512]{3,2,1,0:T(8,128)(2,1)} %bitcast.86) | data formatting | bytes 16777216 | tf_op jit(solution)/shard_map/all_to_all | solution.py:87
  (21 shorter events, 0.1 us)
Async XLA Ops:
  6.5 0.8 copy-start.12
  6.5 2.0 copy-start.11
  6.5 7.5 %copy-start.10 = (f32[2,64]{1,0:T(2,128)S(1)}, f32[2,64]{1,0:T(2,128)}, u32[]{:S(2)}) copy-start(f32[2,64]{1,0:T(2,128)} %param.11) | copy-start | bytes 1540
  6.5 109.1 %all-gather.2.cloned.1.call-start = ((), (), s32[]{:S(2)}) async-start(), calls=%async_computation.1 | async-start | bytes 12582912 | tf_op jit(solution)/shard_map/all_gather | solution.py:44
  7.3 140.1 %all-reduce.4.cloned.1.call-start = ((), (), s32[]{:S(2)}) async-start(), calls=%async_computation.2 | async-start | bytes 1048576 | tf_op jit(solution)/shard_map/psum | solution.py:52
  115.6 5.3 %copy-start.4 = (bf16[2,64,8,2048]{3,2,1,0:T(8,128)(2,1)S(1)}, bf16[2,64,8,2048]{3,2,1,0:T(8,128)(2,1)}, u32[]{:S(2)}) copy-start(bf16[2,64,8,2048]{3,2,1,0:T(8,128)(2,1)} %param.9) | copy-start | bytes 12582916
  121.0 3.2 copy-start
  121.0 5.1 %copy-start.2 = (bf16[64,16,2048]{2,1,0:T(8,128)(2,1)}, bf16[64,16,2048]{2,1,0:T(8,128)(2,1)S(1)}, u32[]{:S(2)}) copy-start(bf16[64,16,2048]{2,1,0:T(8,128)(2,1)S(1)} %get-tuple-element.8) | copy-start | bytes 12582916
  126.1 2.3 copy-start.8
  147.3 3.5 copy-start.3
  147.3 3.5 copy-start.7
  150.9 2.2 copy-start.1
  150.9 3.5 copy-start.5
  154.3 1.0 copy-start.6
  156.3 5.5 %copy-start.9 = (s32[256]{0:T(256)S(1)}, s32[256]{0:T(256)}, u32[]{:S(2)}) copy-start(s32[256]{0:T(256)} %param.13) | copy-start | bytes 3076
  156.7 47.3 %collective-permute-start = (bf16[2,64,8,512]{3,2,1,0:T(8,128)(2,1)S(1)}, bf16[2,64,8,512]{3,2,1,0:T(8,128)(2,1)S(1)}, u32[]{:S(2)}, u32[]{:S(2)}) collective-permute-start(bf16[2,64,8,512]{3,2,1,0:T(8,128)(2,1)S(1)} %get-tuple-element.10), channel_id=1, source_target_pairs={{0,4},{4,0},{8,12},{12,8},{1,5},{5,1},{9,13},{13,9},{2,6},{6,2},{1... | collective-permute-start | bytes 3145736 | tf_op jit(solution)/shard_map/ppermute | solution.py:73
  158.5 71.9 %collective-permute-start.1 = (bf16[2,64,8,512]{3,2,1,0:T(8,128)(2,1)S(1)}, bf16[2,64,8,512]{3,2,1,0:T(8,128)(2,1)S(1)}, u32[]{:S(2)}, u32[]{:S(2)}) collective-permute-start(bf16[2,64,8,512]{3,2,1,0:T(8,128)(2,1)S(1)} %get-tuple-element.11), channel_id=1, source_target_pairs={{0,8},{4,12},{8,0},{12,4},{1,9},{5,13},{9,1},{13,5},{2,10},{6,14},... | collective-permute-start | bytes 3145736 | tf_op jit(solution)/shard_map/ppermute | solution.py:73
  160.9 69.5 %collective-permute-start.2 = (bf16[2,64,8,512]{3,2,1,0:T(8,128)(2,1)S(1)}, bf16[2,64,8,512]{3,2,1,0:T(8,128)(2,1)S(1)}, u32[]{:S(2)}, u32[]{:S(2)}) collective-permute-start(bf16[2,64,8,512]{3,2,1,0:T(8,128)(2,1)S(1)} %get-tuple-element.12), channel_id=1, source_target_pairs={{0,12},{4,8},{8,4},{12,0},{1,13},{5,9},{9,5},{13,1},{2,14},{6,10},... | collective-permute-start | bytes 3145736 | tf_op jit(solution)/shard_map/ppermute | solution.py:73
Sparse Core Ops, SparseCore 0:
  8.9 106.6 all-gather.1
  128.5 18.7 all-reduce.3
